TPU v7x, 256 devices: a whole 4x4x8 slice. The times are simulated.
256 devices in a mesh: row: 16 (over z_lo, x), col: 16 (over z_hi, y, core).
Axes of the slice: x: 4, y: 4, z: 8 (z_hi: 2, z_lo: 4; z = z_hi * 4 + z_lo), core: 2. Of those that a mesh axis runs over, the one named last changes fastest.
Arguments:
- inverse_tiles: bfloat16 [16384, 16384], P('row', 'col'), may hold values from -0.046875 to 0.046875
- factor: bfloat16 [16384, 4, 512], P('row', None, 'col'), may hold values from -0.75 to 0.75
- inverse_diag: float32 [4, 512, 512], P(None, 'row', 'col'), may hold values from -6 to 6
- tile_list: int32 [4, 128], replicated, may hold values from 0 to 127, as said below
- tile_count: int32 [4], replicated, may hold values from 86 to 128, as said below
Outputs:
- inverse_panel: bfloat16 [16384, 4, 512], P(('row', 'col'))
- diag_block: float32 [4, 512, 512], P(None, 'row', 'col')
Inputs may be any that keep to these rules, and one draw needn't show every extreme that they name: For each supernode the first tile_count entries of tile_list name distinct tiles in increasing order; the remaining entries name the tiles that are not listed. `tile_count`: some supernode lists all 128 tiles.
All inputs are finite; a program needn't handle non-finite values.
Results may differ from a plain program's by a relative error of at most 0.014.
Values may be sent and summed in bfloat16 or wider, within the bound.
A program may use at most 64 MiB of HBM per device.

v0:
```python
import jax
import jax.numpy as jnp
from jax import lax
from jax.sharding import Mesh
from jax.sharding import PartitionSpec as P

TILE = 128
COL = ("col_0", "col_1", "col_2")
ROW_COL = ("row", "col_0", "col_1", "col_2")


def spread(x, axis, root):
    mine = lax.axis_index(axis) == root
    return lax.psum(jnp.where(mine, x, jnp.zeros_like(x)), axis)


def split_up(x, dim, size):
    before, after = (x.shape[:dim], x.shape[dim + 1 :])
    return jnp.moveaxis(x.reshape(*before, size, -1, *after), dim, 0)


def summed_rows(x, chips, core, dim):
    sizes = (lax.axis_size(chips), lax.axis_size(core))
    blocks = split_up(x, dim, sizes[0] * sizes[1])
    inside = blocks.shape[1:]
    blocks = blocks.reshape(*sizes, *inside).swapaxes(0, 1).reshape(-1, *inside)
    blocks = lax.psum_scatter(blocks, core, scatter_dimension=0, tiled=True)
    return lax.psum_scatter(blocks, chips, scatter_dimension=0, tiled=True)[0]


def sent_and_summed(x, axis, dim):
    blocks = split_up(x, dim, lax.axis_size(axis))
    arrived = lax.all_to_all(blocks, axis, split_axis=0, concat_axis=0, tiled=True)
    return arrived.astype(jnp.float32).sum(axis=0)


def per_device(inverse_tiles, factor, inverse_diag, tile_list, tile_count):
    row_devices = lax.axis_size("row")
    col_devices = lax.axis_size(COL)
    row_index = lax.axis_index("row")
    col_index = lax.axis_index(COL)
    rows_blk = inverse_tiles.shape[0]
    cols_blk = inverse_tiles.shape[1]
    supers = factor.shape[1]
    panel_width = factor.shape[2] * col_devices
    tile_total = tile_list.shape[1]
    position = jnp.arange(tile_total, dtype=jnp.int32)
    matches = (tile_list[:, :, None] == position[None, None, :]) & (
        position[None, :, None] < tile_count[:, None, None]
    )
    listed = jnp.any(matches, axis=1).astype(jnp.float32)
    live_all = jnp.repeat(listed, TILE, axis=1)
    row_live = lax.dynamic_slice_in_dim(live_all, row_index * rows_blk, rows_blk, 1).T
    row_factor = lax.all_gather(factor, COL, axis=2, tiled=True)
    row_factor = jnp.where(row_live[:, :, None] > 0, row_factor, jnp.zeros_like(row_factor))
    blocks_per = row_devices // col_devices
    received = spread(row_factor, "row", col_index * blocks_per + 0)
    col_factor = received.reshape(cols_blk, supers * panel_width)
    whole_term = jnp.dot(inverse_tiles, col_factor, preferred_element_type=jnp.float32).reshape(
        rows_blk, supers, panel_width
    )
    panel_cols = summed_rows(whole_term, ("col_0", "col_1"), "col_2", 2)
    panel_cols = -panel_cols * row_live[:, :, None]
    diag_part = jnp.einsum(
        "rsv,rsw->svw", row_factor.astype(jnp.float32), panel_cols, precision=lax.Precision.HIGHEST
    )
    diag_mine = sent_and_summed(diag_part.astype(jnp.bfloat16), "row", 1)
    inverse_panel = lax.all_to_all(
        panel_cols.astype(jnp.bfloat16), COL, split_axis=0, concat_axis=2, tiled=True
    )
    diag_block = inverse_diag - diag_mine
    return (inverse_panel, diag_block)


def solution(mesh):
    torus = Mesh(
        mesh.devices.reshape(mesh.shape["row"], 2, 4, 2), ("row", "col_0", "col_1", "col_2")
    )
    return jax.shard_map(
        per_device,
        mesh=torus,
        in_specs=(P("row", COL), P("row", None, COL), P(None, "row", COL), P(), P()),
        out_specs=(P(ROW_COL, None, None), P(None, "row", COL)),
        check_vma=False,
    )
```

profile of v0, /device:TPU:32, one launch (start us, length us, event | category | flops | bytes accessed | tf_op | source)
XLA Modules:
  0.0 482.2 jit_solution(6248333700501249892)
XLA Ops:
  7.2 0.7 all-gather.2.cloned.1.call-update
  8.0 0.7 iota_compare_fusion.1
  8.7 0.9 fusion.6
  9.6 0.1 broadcast_bitcast_fusion
  9.7 0.2 copy.57
  9.9 79.6 %all-gather.2.cloned.1.call-done = bf16[1024,4,512]{0,2,1:T(8,128)(2,1)} async-done(((bf16[1024,4,32]{0,2,1:T(8,128)(2,1)}), bf16[1024,4,512]{0,2,1:T(8,128)(2,1)}) %all-gather.2.cloned.1.call-update) | async-done | bytes 4194320 | tf_op jit(solution)/shard_map/all_gather | solution.py:54
  89.5 4.5 broadcast_select_fusion.1
  94.1 0.0 reduce-scatter.3.cloned.1.call-start
  94.1 169.6 %all-reduce.2.cloned.1.call-done = bf16[1024,2048]{0,1:T(8,128)(2,1)} async-done(((bf16[1024,2048]{0,1:T(8,128)(2,1)}), bf16[1024,2048]{0,1:T(8,128)(2,1)}) %all-reduce.2.cloned.1.call-update) | async-done | bytes 4194320 | tf_op jit(solution)/shard_map/psum | solution.py:14
  263.7 6.4 %fusion.9 = f32[2048,1024]{1,0:T(8,128)S(1)} fusion(bf16[1024,2048]{0,1:T(8,128)(2,1)} %all-reduce.2.cloned.1.call-done, bf16[1024,1024]{1,0:T(8,128)(2,1)S(1)} %copy-done), kind=kOutput, calls=%fused_computation.20 | convolution fusion | flops 4294967296 | bytes 14680064 | tf_op jit(solution)/shard_map/dot_general | solution.py:59
  270.1 4.1 copy.38
  274.2 0.0 reduce-scatter.5.cloned.1.call-start
  274.3 25.8 %reduce-scatter.3.cloned.1.call-done = f32[8,1024,4,32]{1,3,2,0:T(8,128)} async-done(((f32[16,1024,4,32]{1,3,2,0:T(8,128)}), f32[8,1024,4,32]{1,3,2,0:T(8,128)}) %reduce-scatter.3.cloned.1.call-update) | async-done | bytes 4194320 | tf_op jit(solution)/shard_map/reduce_scatter | solution.py:27
  300.1 131.2 %reduce-scatter.5.cloned.1.call-done = f32[1,1024,4,32]{1,3,2,0:T(8,128)} async-done(((f32[8,1024,4,32]{1,3,2,0:T(8,128)}), f32[1,1024,4,32]{1,3,2,0:T(8,128)}) %reduce-scatter.5.cloned.1.call-update) | async-done | bytes 524304 | tf_op jit(solution)/shard_map/reduce_scatter | solution.py:28
  431.3 6.0 %fusion.2 = bf16[4,512,32]{1,2,0:T(8,128)(2,1)S(1)} fusion(bf16[1024,4,512]{0,2,1:T(8,128)(2,1)} %all-gather.2.cloned.1.call-done, pred[1024,4]{0,1:T(4,128)(4,1)S(1)} %get-tuple-element.12, f32[1,1024,4,32]{1,3,2,0:T(8,128)} %reduce-scatter.5.cloned.1.call-done, f32[1024,4]{0,1:T(4,128)S(1)} %get-tuple-element.13), kind=kOutput, calls=%fused_computation.4 | convolution fusion | flops 807731200 | bytes 4870144 | tf_op jit(solution)/shard_map/rsv,rsw->svw/dot_general | solution.py:64
  437.3 0.3 reshape.53
  437.6 0.1 copy.58
  437.7 1.2 reshape.56
  438.9 5.8 %all-to-all-start.1 = ((bf16[16,2,2048]{2,1,0:T(2,128)(2,1)}), bf16[16,2,2048]{2,1,0:T(2,128)(2,1)S(1)}, u32[]{:S(2)}, u32[]{:S(2)}) async-start(bf16[16,2,2048]{2,1,0:T(2,128)(2,1)} %reshape.56), calls=%async_computation.3 | async-start | bytes 262144 | tf_op jit(solution)/shard_map/all_to_all | solution.py:33
  444.7 1.1 fusion.3
  445.8 0.7 copy.39
  446.5 1.7 reshape.54
  448.2 3.4 all-to-all-done.1
  451.6 5.4 %all-to-all-start = ((bf16[16,2,4096]{2,1,0:T(2,128)(2,1)}), bf16[16,2,4096]{2,1,0:T(2,128)(2,1)S(1)}, u32[]{:S(2)}, u32[]{:S(2)}) async-start(bf16[16,2,4096]{2,1,0:T(2,128)(2,1)} %reshape.54), calls=%async_computation.2 | async-start | bytes 524288 | tf_op jit(solution)/shard_map/all_to_all | solution.py:68
  457.0 0.9 copy.45
  457.9 0.3 reshape.57
  458.2 0.1 convert_reduce_fusion
  458.3 0.7 copy.47
  459.1 12.7 %all-to-all-done = bf16[16,2,4096]{2,1,0:T(2,128)(2,1)S(1)} async-done(((bf16[16,2,4096]{2,1,0:T(2,128)(2,1)}), bf16[16,2,4096]{2,1,0:T(2,128)(2,1)S(1)}, u32[]{:S(2)}, u32[]{:S(2)}) %all-to-all-start) | async-done | bytes 262176 | tf_op jit(solution)/shard_map/all_to_all | solution.py:68
  471.8 0.5 reshape.55
  472.3 1.3 copy.50
  473.6 2.0 copy.46
  (10 shorter events, 0.2 us)
Async XLA Ops:
  7.2 256.6 %copy-start = (bf16[1024,1024]{1,0:T(8,128)(2,1)S(1)}, bf16[1024,1024]{1,0:T(8,128)(2,1)}, u32[]{:S(2)}) copy-start(bf16[1024,1024]{1,0:T(8,128)(2,1)} %param.5) | copy-start | bytes 6291460
  7.2 82.4 %all-gather.2.cloned.1.call-start = ((), (), s32[]{:S(2)}) async-start(), calls=%async_computation.4 | async-start | bytes 4456448 | tf_op jit(solution)/shard_map/all_gather | solution.py:54
  7.9 255.8 %all-reduce.2.cloned.1.call-start = ((), (), s32[]{:S(2)}) async-start(), calls=%async_computation.5 | async-start | bytes 8388608 | tf_op jit(solution)/shard_map/psum | solution.py:14
  94.1 206.0 %reduce-scatter.3.cloned.1.call-start = ((), (), s32[]{:S(2)}) async-start(), calls=%async_computation.6 | async-start | bytes 12582912 | tf_op jit(solution)/shard_map/reduce_scatter | solution.py:27
  274.2 157.1 %reduce-scatter.5.cloned.1.call-start = ((), (), s32[]{:S(2)}) async-start(), calls=%async_computation.7 | async-start | bytes 4718592 | tf_op jit(solution)/shard_map/reduce_scatter | solution.py:28
  438.9 12.7 %all-to-all-start.1 = ((bf16[16,2,2048]{2,1,0:T(2,128)(2,1)}), bf16[16,2,2048]{2,1,0:T(2,128)(2,1)S(1)}, u32[]{:S(2)}, u32[]{:S(2)}) async-start(bf16[16,2,2048]{2,1,0:T(2,128)(2,1)} %reshape.56), calls=%async_computation.3 | async-start | bytes 262144 | tf_op jit(solution)/shard_map/all_to_all | solution.py:33
  451.6 20.2 %all-to-all-start = ((bf16[16,2,4096]{2,1,0:T(2,128)(2,1)}), bf16[16,2,4096]{2,1,0:T(2,128)(2,1)S(1)}, u32[]{:S(2)}, u32[]{:S(2)}) async-start(bf16[16,2,4096]{2,1,0:T(2,128)(2,1)} %reshape.54), calls=%async_computation.2 | async-start | bytes 524288 | tf_op jit(solution)/shard_map/all_to_all | solution.py:68
Sparse Core Ops, SparseCore 0:
  10.8 78.7 all-gather.1
  94.2 169.4 all-reduce.1
  274.3 25.6 reduce-scatter.2
  304.6 126.5 reduce-scatter.4
where the time goes:
time: 483 us; the launch traced here: 482 us
  waiting for transfers between devices  423 us (88%)
  local copies, waits for them, and re-layouts  14.1 us (3%)
  between operations  13.9 us (3%)
  matrix products  12.3 us (3%)
  starting transfers between devices  11.4 us (2%)
  other arithmetic  7.39 us (2%)
    psum x1, waiting for transfers between devices, spread(): return lax.psum(jnp.where(mine, x, jnp.zeros_like(x)), axis)  170 us
    reduce_scatter x1, waiting for transfers between devices, summed_rows(): return lax.psum_scatter(blocks, chips, scatter_dimension=0, tiled=True)[0]  131 us
    all_gather x1, waiting for transfers between devices, per_device(): row_factor = lax.all_gather(factor, COL, axis=2, tiled=True)  79.6 us
    reduce_scatter x1, waiting for transfers between devices, summed_rows(): blocks = lax.psum_scatter(blocks, core, scatter_dimension=0, tiled=True)  25.8 us
    all_to_all x1, waiting for transfers between devices, per_device(): lax.all_to_all(panel_cols.astype(jnp.bfloat16), COL, split_axis=0, concat...  12.7 us
  transfers between devices with their start and end apart: 6, of which 6 were waited for; matrix products, arithmetic and copies ran while one was open for 2% of the time, Pallas kernels for 0%

commit v1 on v0

--- a/solution.py
+++ b/solution.py
@@ -65,8 +65,14 @@
         "rsv,rsw->svw", row_factor.astype(jnp.float32), panel_cols, precision=lax.Precision.HIGHEST
     )
     diag_mine = sent_and_summed(diag_part.astype(jnp.bfloat16), "row", 1)
-    inverse_panel = lax.all_to_all(
-        panel_cols.astype(jnp.bfloat16), COL, split_axis=0, concat_axis=2, tiled=True
+    inverse_panel = jnp.concatenate(
+        lax.all_to_all(
+            jnp.stack(jnp.split(panel_cols.astype(jnp.bfloat16), lax.axis_size(COL), axis=0)),
+            COL,
+            0,
+            0,
+        ),
+        axis=2,
     )
     diag_block = inverse_diag - diag_mine
     return (inverse_panel, diag_block)

time: 483 us -> 491 us (1.017)
  local copies, waits for them, and re-layouts: 14.1 us -> 21.1 us
    unnamed x11 -> x28, local copies, waits for them, and re-layouts: 7.55 us -> 15.8 us
  transfers between devices with their start and end apart: 6 -> 6, of which waited for: 6 -> 6; matrix products, arithmetic and copies ran while one was open for 2% -> 1% of each run, Pallas kernels for 0% -> 0%
where the time goes in v1:
time: 491 us; the launch traced here: 490 us
  waiting for transfers between devices  424 us (86%)
  local copies, waits for them, and re-layouts  21.1 us (4%)
  between operations  13.9 us (3%)
  matrix products  12.4 us (3%)
  starting transfers between devices  11.3 us (2%)
  other arithmetic  7.39 us (2%)
    psum x1, waiting for transfers between devices, spread(): return lax.psum(jnp.where(mine, x, jnp.zeros_like(x)), axis)  170 us
    reduce_scatter x1, waiting for transfers between devices, summed_rows(): return lax.psum_scatter(blocks, chips, scatter_dimension=0, tiled=True)[0]  131 us
    all_gather x1, waiting for transfers between devices, per_device(): row_factor = lax.all_gather(factor, COL, axis=2, tiled=True)  79.6 us
    reduce_scatter x1, waiting for transfers between devices, summed_rows(): blocks = lax.psum_scatter(blocks, core, scatter_dimension=0, tiled=True)  25.8 us
    unnamed x28, local copies, waits for them, and re-layouts  15.8 us
    all_to_all x1, waiting for transfers between devices, per_device(): lax.all_to_all(jnp.stack(jnp.split(panel_cols.astype(jnp.bfloat16), lax.a...  13.6 us
  transfers between devices with their start and end apart: 6, of which 6 were waited for; matrix products, arithmetic and copies ran while one was open for 1% of the time, Pallas kernels for 0%

profile of v1, /device:TPU:32, one launch (start us, length us, event | category | flops | bytes accessed | tf_op | source)
XLA Modules:
  0.0 490.3 jit_solution(5882561430228716836)
XLA Ops:
  7.2 0.7 all-gather.2.cloned.1.call-update
  8.0 0.7 iota_compare_fusion.1
  8.7 0.9 fusion.6
  9.9 79.6 %all-gather.2.cloned.1.call-done = bf16[1024,4,512]{0,2,1:T(8,128)(2,1)} async-done(((bf16[1024,4,32]{0,2,1:T(8,128)(2,1)}), bf16[1024,4,512]{0,2,1:T(8,128)(2,1)}) %all-gather.2.cloned.1.call-update) | async-done | bytes 4194320 | tf_op jit(solution)/shard_map/all_gather | solution.py:54
  89.5 4.5 broadcast_select_fusion.1
  94.1 169.6 %all-reduce.2.cloned.1.call-done = bf16[1024,2048]{0,1:T(8,128)(2,1)} async-done(((bf16[1024,2048]{0,1:T(8,128)(2,1)}), bf16[1024,2048]{0,1:T(8,128)(2,1)}) %all-reduce.2.cloned.1.call-update) | async-done | bytes 4194320 | tf_op jit(solution)/shard_map/psum | solution.py:14
  263.7 6.4 %fusion.9 = f32[2048,1024]{1,0:T(8,128)S(1)} fusion(bf16[1024,2048]{0,1:T(8,128)(2,1)} %all-reduce.2.cloned.1.call-done, bf16[1024,1024]{1,0:T(8,128)(2,1)S(1)} %copy-done), kind=kOutput, calls=%fused_computation.53 | convolution fusion | flops 4294967296 | bytes 14680064 | tf_op jit(solution)/shard_map/dot_general | solution.py:59
  270.1 4.1 copy.36
  274.2 25.8 %reduce-scatter.3.cloned.1.call-done = f32[8,1024,4,32]{1,3,2,0:T(8,128)} async-done(((f32[16,1024,4,32]{1,3,2,0:T(8,128)}), f32[8,1024,4,32]{1,3,2,0:T(8,128)}) %reduce-scatter.3.cloned.1.call-update) | async-done | bytes 4194320 | tf_op jit(solution)/shard_map/reduce_scatter | solution.py:27
  300.1 131.5 %reduce-scatter.5.cloned.1.call-done = f32[1,1024,4,32]{1,3,2,0:T(8,128)} async-done(((f32[8,1024,4,32]{1,3,2,0:T(8,128)}), f32[1,1024,4,32]{1,3,2,0:T(8,128)}) %reduce-scatter.5.cloned.1.call-update) | async-done | bytes 524304 | tf_op jit(solution)/shard_map/reduce_scatter | solution.py:28
  431.5 1.1 fusion.3
  432.6 0.6 constant_dynamic-update-slice_fusion.15
  433.3 0.7 constant_dynamic-update-slice_fusion.14
  434.6 0.7 constant_dynamic-update-slice_fusion.12
  435.3 0.6 constant_dynamic-update-slice_fusion.11
  435.9 0.7 constant_dynamic-update-slice_fusion.10
  437.2 0.7 constant_dynamic-update-slice_fusion.8
  438.5 0.7 constant_dynamic-update-slice_fusion.6
  439.8 0.7 constant_dynamic-update-slice_fusion.4
  440.5 0.6 constant_dynamic-update-slice_fusion.3
  441.2 0.7 constant_dynamic-update-slice_fusion.2
  441.8 6.0 %fusion.2 = bf16[4,512,32]{1,2,0:T(8,128)(2,1)S(1)} fusion(bf16[1024,4,512]{0,2,1:T(8,128)(2,1)} %all-gather.2.cloned.1.call-done, pred[1024,4]{0,1:T(4,128)(4,1)S(1)} %get-tuple-element.8, f32[1,1024,4,32]{1,3,2,0:T(8,128)} %reduce-scatter.5.cloned.1.call-done, f32[1024,4]{0,1:T(4,128)S(1)} %get-tuple-element.9), kind=kOutput, calls=%fused_computation.4 | convolution fusion | flops 807731200 | bytes 4870144 | tf_op jit(solution)/shard_map/rsv,rsw->svw/dot_general | solution.py:64
  448.3 1.2 reshape.64
  449.5 5.8 %all-to-all-start.1 = ((bf16[16,2,2048]{2,1,0:T(2,128)(2,1)}), bf16[16,2,2048]{2,1,0:T(2,128)(2,1)S(1)}, u32[]{:S(2)}, u32[]{:S(2)}) async-start(bf16[16,2,2048]{2,1,0:T(2,128)(2,1)} %reshape.64), calls=%async_computation.3 | async-start | bytes 262144 | tf_op jit(solution)/shard_map/all_to_all | solution.py:33
  455.3 0.6 constant_dynamic-update-slice_fusion.1
  455.9 0.7 constant_dynamic-update-slice_fusion
  456.6 2.1 reshape.62
  458.8 3.5 all-to-all-done.1
  462.2 5.4 %all-to-all-start = ((bf16[16,2,4096]{2,1,0:T(2,128)(2,1)}), bf16[16,2,4096]{2,1,0:T(2,128)(2,1)S(1)}, u32[]{:S(2)}, u32[]{:S(2)}) async-start(bf16[16,2,4096]{2,1,0:T(2,128)(2,1)} %reshape.62), calls=%async_computation.2 | async-start | bytes 524288 | tf_op jit(solution)/shard_map/all_to_all | solution.py:69
  468.1 0.7 copy.43
  468.8 13.6 %all-to-all-done = bf16[16,2,4096]{2,1,0:T(2,128)(2,1)S(1)} async-done(((bf16[16,2,4096]{2,1,0:T(2,128)(2,1)}), bf16[16,2,4096]{2,1,0:T(2,128)(2,1)S(1)}, u32[]{:S(2)}, u32[]{:S(2)}) %all-to-all-start) | async-done | bytes 262176 | tf_op jit(solution)/shard_map/all_to_all | solution.py:69
  482.8 1.0 copy.42
  (28 shorter events, 4.3 us)
Async XLA Ops:
  7.2 256.6 %copy-start = (bf16[1024,1024]{1,0:T(8,128)(2,1)S(1)}, bf16[1024,1024]{1,0:T(8,128)(2,1)}, u32[]{:S(2)}) copy-start(bf16[1024,1024]{1,0:T(8,128)(2,1)} %param.5) | copy-start | bytes 6291460
  7.2 82.4 %all-gather.2.cloned.1.call-start = ((), (), s32[]{:S(2)}) async-start(), calls=%async_computation.4 | async-start | bytes 4456448 | tf_op jit(solution)/shard_map/all_gather | solution.py:54
  7.9 255.8 %all-reduce.2.cloned.1.call-start = ((), (), s32[]{:S(2)}) async-start(), calls=%async_computation.5 | async-start | bytes 8388608 | tf_op jit(solution)/shard_map/psum | solution.py:14
  94.1 205.9 %reduce-scatter.3.cloned.1.call-start = ((), (), s32[]{:S(2)}) async-start(), calls=%async_computation.6 | async-start | bytes 12582912 | tf_op jit(solution)/shard_map/reduce_scatter | solution.py:27
  274.2 157.3 %reduce-scatter.5.cloned.1.call-start = ((), (), s32[]{:S(2)}) async-start(), calls=%async_computation.7 | async-start | bytes 4718592 | tf_op jit(solution)/shard_map/reduce_scatter | solution.py:28
  441.8 25.8 %copy-start.1 = (f32[4,32,32]{2,1,0:T(8,128)S(1)}, f32[4,32,32]{2,1,0:T(8,128)}, u32[]{:S(2)}) copy-start(f32[4,32,32]{2,1,0:T(8,128)} %param.7) | copy-start | bytes 49156
  449.5 12.7 %all-to-all-start.1 = ((bf16[16,2,2048]{2,1,0:T(2,128)(2,1)}), bf16[16,2,2048]{2,1,0:T(2,128)(2,1)S(1)}, u32[]{:S(2)}, u32[]{:S(2)}) async-start(bf16[16,2,2048]{2,1,0:T(2,128)(2,1)} %reshape.64), calls=%async_computation.3 | async-start | bytes 262144 | tf_op jit(solution)/shard_map/all_to_all | solution.py:33
  462.2 20.2 %all-to-all-start = ((bf16[16,2,4096]{2,1,0:T(2,128)(2,1)}), bf16[16,2,4096]{2,1,0:T(2,128)(2,1)S(1)}, u32[]{:S(2)}, u32[]{:S(2)}) async-start(bf16[16,2,4096]{2,1,0:T(2,128)(2,1)} %reshape.62), calls=%async_computation.2 | async-start | bytes 524288 | tf_op jit(solution)/shard_map/all_to_all | solution.py:69
Sparse Core Ops, SparseCore 0:
  10.8 78.7 all-gather.1
  94.2 169.4 all-reduce.1
  274.3 25.6 reduce-scatter.2
  304.6 126.8 reduce-scatter.4
